TPU v7x, 32 devices: a whole 2x2x4 slice. The times are simulated.
32 devices in a mesh: groups: 2 (over y), tensor: 8 (over z, x), dp: 2 (over core).
Axes of the slice: x: 2, y: 2, z: 4, core: 2. Of those that a mesh axis runs over, the one named last changes fastest.
Arguments:
- layer_inputs: bfloat16 [16384, 8192], P(('groups', 'dp'), 'tensor'), parts along dimension 0, may hold values from -6 to 6
- output_grads: bfloat16 [16384, 28672], P(('groups', 'dp'), 'tensor'), parts along dimension 0, may hold values from -6 to 6
- proj_in: bfloat16 [8192, 64], P('tensor'), may hold values from -0.0625 to 0.0625
- proj_out: bfloat16 [28672, 64], P('tensor'), may hold values from -0.03125 to 0.03125
- inv_out: float32 [64, 64], replicated, may hold values from -0.3 to 4, as said below
- inv_in: float32 [64, 64], replicated, may hold values from -0.3 to 4, as said below
- stored: bfloat16 [2560, 4096], P(('groups', 'tensor', 'dp')), parts along dimension 0, may hold values from -0.01171875 to 0.01171875
- lengths: int32 [4, 64], P(('groups', 'dp')), parts along dimension 0, may hold values from 1 to 128, 4096 in all within a row
Outputs:
- scores: float32 [1280, 256], P(('tensor', 'dp'), 'groups'), parts along dimension 1
There are 2 independent parts, one for each index of `groups`. A program takes and returns all parts, laid end to end along the dimension named above; an argument that names none is the same for every part. Nothing has to cross between parts.
Inputs may be any that keep to these rules, and one draw needn't show every extreme that they name: `lengths`: each row sums to 4096. `inv_out`: Symmetric. `inv_in`: Symmetric.
All inputs are finite; a program needn't handle non-finite values.
Results may differ from a plain program's by a relative error of at most 0.005.
Values may be sent and summed in bfloat16 or wider, within the bound.
A program may use at most 128 MiB of HBM per device.

v0:
```python
import jax
import jax.numpy as jnp
from jax import lax
from jax.sharding import PartitionSpec as P


def segment_outer(grad_rows, input_rows, starts, ends, first):
    positions = first + lax.iota(jnp.int32, grad_rows.shape[0])
    member = (
        (positions[None, :] >= starts[:, None]) & (positions[None, :] < ends[:, None])
    ).astype(jnp.bfloat16)
    grad_cols = grad_rows.T
    weighted = member[:, None, :] * grad_cols[None, :, :]
    outer = jnp.einsum("ert,ts->ers", weighted, input_rows, preferred_element_type=jnp.float32)
    return outer.reshape(outer.shape[0], -1)


def blockwise_sketch(grad_all, input_all, starts, ends):
    tok_rows = grad_all.shape[0]
    rank = grad_all.shape[1]
    block = min(512, tok_rows)
    num_blocks = tok_rows // block
    grad_blocks = grad_all.reshape(num_blocks, block, rank)
    input_blocks = input_all.reshape(num_blocks, block, rank)
    offsets = lax.iota(jnp.int32, num_blocks) * block

    def step(total, items):
        grad_block, input_block, offset = items
        return (total + segment_outer(grad_block, input_block, starts, ends, offset), None)

    initial = jnp.zeros((starts.shape[0], rank * rank), jnp.float32)
    total, unused = lax.scan(step, initial, (grad_blocks, input_blocks, offsets))
    return total


def precondition(inv_out, flat_sketch, inv_in):
    rank = inv_out.shape[0]
    square = flat_sketch.reshape(flat_sketch.shape[0], rank, rank)
    result = jnp.einsum("ab,ebc,cd->ead", inv_out, square, inv_in, precision=lax.Precision.HIGHEST)
    return result.reshape(flat_sketch.shape[0], rank * rank)


def project_rows(layer_inputs, output_grads, proj_in, proj_out):
    return jnp.concatenate(
        [
            jnp.dot(layer_inputs, proj_in, preferred_element_type=jnp.float32),
            jnp.dot(output_grads, proj_out, preferred_element_type=jnp.float32),
        ],
        axis=1,
    )


def on_device(layer_inputs, output_grads, proj_in, proj_out, inv_out, inv_in, stored, lengths):
    rank = proj_in.shape[1]
    counts = lengths[0]
    ends = jnp.cumsum(counts)
    starts = ends - counts
    both_sums = lax.psum(
        project_rows(layer_inputs, output_grads, proj_in, proj_out), "tensor"
    ).astype(jnp.bfloat16)
    sketch = blockwise_sketch(both_sums[:, rank:], both_sums[:, :rank], starts, ends)
    query = precondition(inv_out, sketch, inv_in).astype(jnp.bfloat16)
    return lax.dot_general(
        stored,
        lax.all_gather(query, "dp", axis=0, tiled=True),
        (((1,), (1,)), ((), ())),
        preferred_element_type=jnp.float32,
    )


def solution(mesh):
    placed = (
        P(("groups", "dp"), "tensor"),
        P(("groups", "dp"), "tensor"),
        P("tensor", None),
        P("tensor", None),
        P(),
        P(),
        P(("groups", "tensor", "dp"), None),
        P(("groups", "dp"), None),
    )
    return jax.shard_map(
        on_device,
        mesh=mesh,
        in_specs=placed,
        out_specs=P(("tensor", "dp"), "groups"),
        check_vma=False,
    )
```

profile of v0, /device:TPU:0, one launch (start us, length us, event | category | flops | bytes accessed | tf_op | source)
XLA Modules:
  0.0 217.8 jit_solution(17159385210420608280)
XLA Ops:
  6.6 6.1 %fusion.11 = f32[4096,64]{0,1:T(8,128)S(1)} fusion(bf16[4096,1024]{1,0:T(8,128)(2,1)} %param.10, bf16[1024,64]{0,1:T(8,128)(2,1)} %param.12), kind=kOutput, calls=%fused_computation.22 | convolution fusion | flops 536870912 | bytes 9568256 | tf_op jit(solution)/shard_map/dot_general | solution.py:46
  12.7 14.2 %fusion.12 = f32[4096,64]{0,1:T(8,128)S(1)} fusion(bf16[4096,3584]{1,0:T(8,128)(2,1)} %param.11, bf16[3584,64]{0,1:T(8,128)(2,1)S(1)} %copy-done.1), kind=kOutput, calls=%fused_computation.23 | convolution fusion | flops 1879048192 | bytes 30867456 | tf_op jit(solution)/shard_map/dot_general | solution.py:47
  26.9 1.5 pad_maximum_fusion
  28.4 94.7 %all-reduce.1 = bf16[4096,128]{0,1:T(8,128)(2,1)S(1)} all-reduce(f32[4096,128]{0,1:T(8,128)} %pad_maximum_fusion), channel_id=1, replica_groups=mesh['groups'=2,'tensor'=8,'dp'=2] {'tensor'}, use_global_device_ids=true, to_apply=%region_0.0 | all-reduce | flops 524288 | bytes 3145728 | tf_op jit(solution)/shard_map/psum | solution.py:58
  123.1 0.9 fusion.10
  124.3 2.2 copy_bitcast_fusion
  126.5 65.1 %while.11 = (s32[]{:T(128)}, f32[64,4096]{1,0:T(8,128)S(1)}, s32[8]{0:T(128)S(1)}, s32[64]{0:T(128)S(1)}, s32[64]{0:T(128)S(1)}, /*index=5*/bf16[8,512,64]{1,2,0...) while((s32[]{:T(128)}, f32[64,4096]{1,0:T(8,128)S(1)}, s32[8]{0:T(128)S(1)}, ...), condition=%wide.region_3.4_spmd.clone, body=%wide.region_2.3_spmd.clone.sunk | while | flops 271188480 | bytes 6689915 | solution.py:32
  128.7 3.4 %fusion.26 = f32[64,64,64]{2,1,0:T(8,128)} fusion(bf16[64,512]{1,0:T(8,128)(2,1)S(1)} %dynamic-slice_bitcast_fusion.2, bf16[64,512]{1,0:T(8,128)(2,1)S(1)} %and_convert_fusion.2, bf16[8,512,64]{1,2,0:T(8,128)(2,1)} %get-tuple-element.166, s32[]{:T(128)} %get-tuple-element.151), kind=kOutput, calls=%fused_computation.clone.1 | convolution fusion | flops 270532608 | bytes 1245696 | tf_op jit(solution)/shard_map/while/body/eval_jaxpr/ert,ts->ers/dot_general | solution.py:14
  132.1 2.1 reshape.105
  136.9 3.4 %fusion.26 = f32[64,64,64]{2,1,0:T(8,128)} fusion(bf16[64,512]{1,0:T(8,128)(2,1)S(1)} %dynamic-slice_bitcast_fusion.2, bf16[64,512]{1,0:T(8,128)(2,1)S(1)} %and_convert_fusion.2, bf16[8,512,64]{1,2,0:T(8,128)(2,1)} %get-tuple-element.166, s32[]{:T(128)} %get-tuple-element.151), kind=kOutput, calls=%fused_computation.clone.1 | convolution fusion | flops 270532608 | bytes 1245696 | tf_op jit(solution)/shard_map/while/body/eval_jaxpr/ert,ts->ers/dot_general | solution.py:14
  140.3 2.1 reshape.105
  145.0 3.4 %fusion.26 = f32[64,64,64]{2,1,0:T(8,128)} fusion(bf16[64,512]{1,0:T(8,128)(2,1)S(1)} %dynamic-slice_bitcast_fusion.2, bf16[64,512]{1,0:T(8,128)(2,1)S(1)} %and_convert_fusion.2, bf16[8,512,64]{1,2,0:T(8,128)(2,1)} %get-tuple-element.166, s32[]{:T(128)} %get-tuple-element.151), kind=kOutput, calls=%fused_computation.clone.1 | convolution fusion | flops 270532608 | bytes 1245696 | tf_op jit(solution)/shard_map/while/body/eval_jaxpr/ert,ts->ers/dot_general | solution.py:14
  148.4 2.1 reshape.105
  153.1 3.4 %fusion.26 = f32[64,64,64]{2,1,0:T(8,128)} fusion(bf16[64,512]{1,0:T(8,128)(2,1)S(1)} %dynamic-slice_bitcast_fusion.2, bf16[64,512]{1,0:T(8,128)(2,1)S(1)} %and_convert_fusion.2, bf16[8,512,64]{1,2,0:T(8,128)(2,1)} %get-tuple-element.166, s32[]{:T(128)} %get-tuple-element.151), kind=kOutput, calls=%fused_computation.clone.1 | convolution fusion | flops 270532608 | bytes 1245696 | tf_op jit(solution)/shard_map/while/body/eval_jaxpr/ert,ts->ers/dot_general | solution.py:14
  156.6 2.1 reshape.105
  160.4 0.9 dynamic-slice_bitcast_fusion.2
  161.3 3.4 %fusion.26 = f32[64,64,64]{2,1,0:T(8,128)} fusion(bf16[64,512]{1,0:T(8,128)(2,1)S(1)} %dynamic-slice_bitcast_fusion.2, bf16[64,512]{1,0:T(8,128)(2,1)S(1)} %and_convert_fusion.2, bf16[8,512,64]{1,2,0:T(8,128)(2,1)} %get-tuple-element.166, s32[]{:T(128)} %get-tuple-element.151), kind=kOutput, calls=%fused_computation.clone.1 | convolution fusion | flops 270532608 | bytes 1245696 | tf_op jit(solution)/shard_map/while/body/eval_jaxpr/ert,ts->ers/dot_general | solution.py:14
  164.7 2.1 reshape.105
  168.6 0.9 dynamic-slice_bitcast_fusion.2
  169.4 3.4 %fusion.26 = f32[64,64,64]{2,1,0:T(8,128)} fusion(bf16[64,512]{1,0:T(8,128)(2,1)S(1)} %dynamic-slice_bitcast_fusion.2, bf16[64,512]{1,0:T(8,128)(2,1)S(1)} %and_convert_fusion.2, bf16[8,512,64]{1,2,0:T(8,128)(2,1)} %get-tuple-element.166, s32[]{:T(128)} %get-tuple-element.151), kind=kOutput, calls=%fused_computation.clone.1 | convolution fusion | flops 270532608 | bytes 1245696 | tf_op jit(solution)/shard_map/while/body/eval_jaxpr/ert,ts->ers/dot_general | solution.py:14
  172.9 2.1 reshape.105
  176.7 0.9 dynamic-slice_bitcast_fusion.2
  177.6 3.4 %fusion.26 = f32[64,64,64]{2,1,0:T(8,128)} fusion(bf16[64,512]{1,0:T(8,128)(2,1)S(1)} %dynamic-slice_bitcast_fusion.2, bf16[64,512]{1,0:T(8,128)(2,1)S(1)} %and_convert_fusion.2, bf16[8,512,64]{1,2,0:T(8,128)(2,1)} %get-tuple-element.166, s32[]{:T(128)} %get-tuple-element.151), kind=kOutput, calls=%fused_computation.clone.1 | convolution fusion | flops 270532608 | bytes 1245696 | tf_op jit(solution)/shard_map/while/body/eval_jaxpr/ert,ts->ers/dot_general | solution.py:14
  181.0 2.1 reshape.105
  185.7 3.4 %fusion.26 = f32[64,64,64]{2,1,0:T(8,128)} fusion(bf16[64,512]{1,0:T(8,128)(2,1)S(1)} %dynamic-slice_bitcast_fusion.2, bf16[64,512]{1,0:T(8,128)(2,1)S(1)} %and_convert_fusion.2, bf16[8,512,64]{1,2,0:T(8,128)(2,1)} %get-tuple-element.166, s32[]{:T(128)} %get-tuple-element.151), kind=kOutput, calls=%fused_computation.clone.1 | convolution fusion | flops 270532608 | bytes 1245696 | tf_op jit(solution)/shard_map/while/body/eval_jaxpr/ert,ts->ers/dot_general | solution.py:14
  189.1 2.1 reshape.105
  191.6 2.2 reshape.98
  193.8 3.6 %fusion.8 = f32[64,64,64]{1,2,0:T(8,128)S(1)} fusion(f32[64,64,64]{2,1,0:T(8,128)} %reshape.98, f32[64,64]{1,0:T(8,128)S(1)} %copy-done.2), kind=kOutput, calls=%fused_computation.17 | convolution fusion | flops 201326592 | bytes 2113536 | tf_op jit(solution)/shard_map/ab,ebc,cd->ead/dot_general | solution.py:39
  197.4 1.8 convolution_convert_fusion
  199.2 1.6 convert_element_type.18
  200.8 7.8 %all-gather.2.cloned.1.call-done = bf16[128,4096]{1,0:T(8,128)(2,1)} async-done(((bf16[64,4096]{1,0:T(8,128)(2,1)}), bf16[128,4096]{1,0:T(8,128)(2,1)}) %all-gather.2.cloned.1.call-update) | async-done | bytes 1048592 | tf_op jit(solution)/shard_map/all_gather | solution.py:65
  208.6 2.3 %convolution_bitcast_fusion = f32[80,128]{1,0:T(8,128)} fusion(bf16[128,4096]{1,0:T(8,128)(2,1)} %all-gather.2.cloned.1.call-done, bf16[80,4096]{1,0:T(8,128)(2,1)S(1)} %copy-done), kind=kOutput, calls=%fused_computation.13 | convolution fusion | flops 83886080 | bytes 1744896 | tf_op jit(solution)/shard_map/dot_general | solution.py:63
  (55 shorter events, 18.2 us)
Async XLA Ops:
  6.5 202.1 %copy-start = (bf16[80,4096]{1,0:T(8,128)(2,1)S(1)}, bf16[80,4096]{1,0:T(8,128)(2,1)}, u32[]{:S(2)}) copy-start(bf16[80,4096]{1,0:T(8,128)(2,1)} %param.16) | copy-start | bytes 1966084
  6.5 202.1 %all-gather.2.cloned.1.call-start = ((), (), s32[]{:S(2)}) async-start(), calls=%async_computation | async-start | bytes 1572864 | tf_op jit(solution)/shard_map/all_gather | solution.py:65
  6.5 6.1 %copy-start.1 = (bf16[3584,64]{0,1:T(8,128)(2,1)S(1)}, bf16[3584,64]{0,1:T(8,128)(2,1)}, u32[]{:S(2)}) copy-start(bf16[3584,64]{0,1:T(8,128)(2,1)} %param.13) | copy-start | bytes 1376260
  28.4 95.6 %copy-start.4 = (s32[1,64]{1,0:T(1,128)S(1)}, s32[1,64]{1,0:T(1,128)}, u32[]{:S(2)}) copy-start(s32[1,64]{1,0:T(1,128)} %param.17) | copy-start | bytes 772
  191.6 2.2 %copy-start.2 = (f32[64,64]{1,0:T(8,128)S(1)}, f32[64,64]{1,0:T(8,128)}, u32[]{:S(2)}) copy-start(f32[64,64]{1,0:T(8,128)} %param.14) | copy-start | bytes 49156
  193.8 3.6 %copy-start.3 = (f32[64,64]{1,0:T(8,128)S(1)}, f32[64,64]{1,0:T(8,128)}, u32[]{:S(2)}) copy-start(f32[64,64]{1,0:T(8,128)} %param.15) | copy-start | bytes 49156
Sparse Core Ops, SparseCore 0:
  201.0 7.5 all-gather.1
where the time goes:
time: 219 us; the launch traced here: 218 us
  blocking collectives  94.7 us (43%)
  matrix products  55.4 us (25%)
  local copies, waits for them, and re-layouts  36 us (16%)
  between operations  13.5 us (6%)
  other arithmetic  10.1 us (5%)
  waiting for transfers between devices  7.77 us (4%)
    psum x1, blocking collectives, on_device(): lax.psum(project_rows(layer_inputs, output_grads, proj_in, proj_out), 'te...  94.7 us
    dot_general x8, matrix products, segment_outer(): jnp.einsum('ert,ts->ers', weighted, input_rows, preferred_element_type=jn...  27.3 us
    reshape x8, local copies, waits for them, and re-layouts, segment_outer(): return outer.reshape(outer.shape[0], -1)  17 us
    dot_general x1, matrix products, project_rows(): jnp.dot(output_grads, proj_out, preferred_element_type=jnp.float32)  14.2 us
    all_gather x1, waiting for transfers between devices, on_device(): lax.all_gather(query, 'dp', axis=0, tiled=True)  7.76 us
    transpose x8, local copies, waits for them, and re-layouts, segment_outer(): grad_cols = grad_rows.T  6.81 us
    dot_general x1, matrix products, project_rows(): jnp.dot(layer_inputs, proj_in, preferred_element_type=jnp.float32)  6.13 us
    dot_general x2, matrix products, precondition(): jnp.einsum('ab,ebc,cd->ead', inv_out, square, inv_in, precision=lax.Preci...  5.36 us
  transfers between devices with their start and end apart: 1, of which 1 were waited for; matrix products, arithmetic and copies ran while one was open for 0% of the time, Pallas kernels for 0%

commit v1 on v0

v1 whole, which is shorter than its diff:
```python
import functools
import jax
import jax.numpy as jnp
from jax import lax
from jax.experimental import pallas as pl
from jax.experimental.pallas import tpu as pltpu
from jax.sharding import PartitionSpec as P

MESH = pl.DeviceIdType.MESH
LONGEST = 128
WIRE_X = jnp.float32
WIRE_Z = jnp.float32
AHEAD = 3
LAG = 1


def window_of(total):
    return min(total, LONGEST + 16)


def inner_size(count):
    inner = 1
    while (2 * inner) ** 3 <= count:
        inner *= 2
    return inner


def token_kernel(
    outer, inner,
    x_hbm, g_hbm, w_in, w_out,
    tokens_out,
    x_buf, g_buf, w_x, w_g, own, send_x, recv_x, send_z, recv_z,
    tokens,
    load_sem, sx_sem, rx_sem, sz_sem, rz_sem, gz_send, gz_recv, gx_send, gx_recv,
):
    parts = outer * inner
    total = x_buf.shape[0]
    chunk = total // parts
    rank = w_in.shape[1]
    wide = 2 * rank
    me = lax.axis_index("tensor")
    my_o = me // inner
    my_i = me % inner

    def rows_of(o, i):
        return pl.ds(pl.multiple_of((o * inner + i) * chunk, chunk), chunk)

    order = []
    for s in range(outer):
        o = lax.rem(my_o + 1 + s, outer)
        for r in list(range(1, inner)) + [0]:
            order.append((s, r, o, lax.rem(my_i + r, inner)))

    def loads(k):
        _, _, o, i = order[k]
        rows = rows_of(o, i)
        return (
            pltpu.make_async_copy(x_hbm.at[rows], x_buf.at[rows], load_sem.at[0, k]),
            pltpu.make_async_copy(g_hbm.at[rows], g_buf.at[rows], load_sem.at[1, k]),
        )

    for k in range(min(AHEAD, parts)):
        for copy in loads(k):
            copy.start()

    barrier = pltpu.get_barrier_semaphore()
    peers = [{"tensor": lax.rem(my_o + s, outer) * inner + my_i} for s in range(1, outer)]
    peers += [{"tensor": my_o * inner + lax.rem(my_i + r, inner)} for r in range(1, inner)]
    for peer in peers:
        pl.semaphore_signal(barrier, inc=1, device_id=peer, device_id_type=MESH)

    w_x[...] = jnp.concatenate([w_in[...], jnp.zeros_like(w_in)], axis=1)
    w_g[...] = jnp.concatenate([jnp.zeros_like(w_out), w_out[...]], axis=1)
    pl.semaphore_wait(barrier, len(peers))

    sub = min(256, chunk)

    def project(k, dest):
        _, _, o, i = order[k]
        for copy in loads(k):
            copy.wait()
        if k + AHEAD < parts:
            for copy in loads(k + AHEAD):
                copy.start()
        base = (o * inner + i) * chunk

        @pl.loop(0, chunk // sub)
        def _(h):
            rows = pl.ds(pl.multiple_of(base + h * sub, sub), sub)
            value = jnp.dot(x_buf[rows, :], w_x[...], preferred_element_type=jnp.float32)
            value += jnp.dot(g_buf[rows, :], w_g[...], preferred_element_type=jnp.float32)
            dest[pl.ds(pl.multiple_of(h * sub, sub), sub), :] = value.astype(dest.dtype)

    def x_copy(s, r):
        return pltpu.make_async_remote_copy(
            src_ref=send_x.at[s, r - 1], dst_ref=recv_x.at[s, r - 1],
            send_sem=sx_sem.at[s, r - 1], recv_sem=rx_sem.at[s, r - 1],
            device_id={"tensor": my_o * inner + lax.rem(my_i + r, inner)}, device_id_type=MESH,
        )

    def z_copy(s):
        return pltpu.make_async_remote_copy(
            src_ref=send_z.at[s], dst_ref=recv_z.at[s],
            send_sem=sz_sem.at[s], recv_sem=rz_sem.at[s],
            device_id={"tensor": lax.rem(my_o + 1 + s, outer) * inner + my_i}, device_id_type=MESH,
        )

    def combine(s):
        value = own[s]
        for r in range(1, inner):
            x_copy(s, r).wait_recv()
            value = value + recv_x[s, r - 1].astype(jnp.float32)
        if s < outer - 1:
            send_z[s] = value.astype(send_z.dtype)
            z_copy(s).start()
        else:
            for q in range(outer - 1):
                z_copy(q).wait_recv()
                value = value + recv_z[q].astype(jnp.float32)
            tokens[rows_of(my_o, my_i), :] = value.astype(tokens.dtype)

    for k in range(parts):
        s, r, _, _ = order[k]
        if r:
            project(k, send_x.at[s, r - 1])
            x_copy(s, r).start()
        else:
            project(k, own.at[s])
            if s >= LAG:
                combine(s - LAG)
    for s in range(outer - min(LAG, outer), outer):
        combine(s)

    def gather_z(s):
        rows = rows_of(my_o, my_i)
        return pltpu.make_async_remote_copy(
            src_ref=tokens.at[rows], dst_ref=tokens.at[rows],
            send_sem=gz_send.at[s], recv_sem=gz_recv.at[s],
            device_id={"tensor": lax.rem(my_o + 1 + s, outer) * inner + my_i}, device_id_type=MESH,
        )

    def gather_x(s, r):
        rows = rows_of(lax.rem(my_o + outer - s, outer), my_i)
        return pltpu.make_async_remote_copy(
            src_ref=tokens.at[rows], dst_ref=tokens.at[rows],
            send_sem=gx_send.at[s, r - 1], recv_sem=gx_recv.at[s, r - 1],
            device_id={"tensor": my_o * inner + lax.rem(my_i + r, inner)}, device_id_type=MESH,
        )

    for s in range(outer - 1):
        gather_z(s).start()
    for r in range(1, inner):
        gather_x(0, r).start()
    for s in range(outer - 1):
        gather_z(s).wait_recv()
        for r in range(1, inner):
            gather_x(s + 1, r).start()
    for s in range(outer):
        for r in range(1, inner):
            gather_x(s, r).wait_recv()

    for s in range(outer):
        for r in range(1, inner):
            x_copy(s, r).wait_send()
            gather_x(s, r).wait_send()
    for s in range(outer - 1):
        z_copy(s).wait_send()
        gather_z(s).wait_send()
    tokens_out[...] = tokens[...]


def sketch_kernel(tokens, bounds, query, sketch):
    total, wide = tokens.shape
    rank = wide // 2
    examples = bounds.shape[1]
    window = window_of(total)
    row = lax.broadcasted_iota(jnp.int32, (window, wide), 0)
    left = lax.broadcasted_iota(jnp.int32, (window, wide), 1) < rank

    def example(e, carry):
        first = pl.multiple_of(bounds[0, e], 16)
        rows = tokens[pl.ds(first, window), :]
        wide_rows = rows.astype(jnp.float32)
        twice = jnp.where(left, wide_rows, pltpu.roll(wide_rows, rank, 1))
        inside = (row >= bounds[1, e]) & (row < bounds[2, e])
        picked = jnp.where(inside, twice, 0.0).astype(jnp.bfloat16)
        outer_product = lax.dot_general(
            rows, picked, (((0,), (0,)), ((), ())), preferred_element_type=jnp.float32
        )
        sketch[pl.ds(pl.multiple_of(e * rank, rank), rank), :] = outer_product[rank:, :]
        return carry

    lax.fori_loop(0, examples, example, 0, unroll=4)

    low = lax.broadcasted_iota(jnp.int32, (examples, wide), 1) < rank
    for a in range(0, rank, 2):
        pair = jnp.where(
            low,
            sketch[pl.ds(a, examples, stride=rank), :],
            sketch[pl.ds(a + 1, examples, stride=rank), :],
        )
        query[:, a * rank:(a + 2) * rank] = pair.astype(query.dtype)


def score_kernel(stored, query, out, both, pair_send, pair_recv):
    core = lax.axis_index("dp")
    examples = query.shape[0]
    barrier = pltpu.get_barrier_semaphore()
    pl.semaphore_signal(barrier, inc=1, device_id={"dp": 1 - core}, device_id_type=MESH)
    mine = pl.ds(pl.multiple_of(core * examples, examples), examples)
    both[mine, :] = query[...]
    pl.semaphore_wait(barrier, 1)
    swap = pltpu.make_async_remote_copy(
        src_ref=query, dst_ref=both.at[mine],
        send_sem=pair_send, recv_sem=pair_recv,
        device_id={"dp": 1 - core}, device_id_type=MESH,
    )
    swap.start()
    swap.wait()
    out[...] = lax.dot_general(
        stored[...], both[...], (((1,), (1,)), ((), ())), preferred_element_type=jnp.float32
    )


def on_device(parts, cores, layer_inputs, output_grads, proj_in, proj_out, inv_out, inv_in, stored, lengths):
    total, depth_in = layer_inputs.shape
    depth_out = output_grads.shape[1]
    rank = proj_in.shape[1]
    wide = 2 * rank
    inner = inner_size(parts)
    outer = parts // inner
    chunk = total // parts
    examples = lengths.shape[1]
    count = stored.shape[0]
    square = stored.astype(jnp.float32).reshape(count, rank, rank)
    moved = jnp.einsum("ac,jab,db->jcd", inv_out, square, inv_in, precision=lax.Precision.HIGHEST)
    moved = moved.reshape(count, rank * rank).astype(jnp.bfloat16)
    ends = jnp.cumsum(lengths[0])
    begins = ends - lengths[0]
    firsts = jnp.minimum((begins // 16) * 16, total - window_of(total))
    bounds = jnp.stack([firsts, begins - firsts, ends - firsts])
    vmem = pl.BlockSpec(memory_space=pltpu.VMEM)
    dma = pltpu.SemaphoreType.DMA
    tokens = pl.pallas_call(
        functools.partial(token_kernel, outer, inner),
        out_shape=jax.ShapeDtypeStruct((total, wide), jnp.bfloat16),
        in_specs=[pl.BlockSpec(memory_space=pl.ANY), pl.BlockSpec(memory_space=pl.ANY), vmem, vmem],
        out_specs=vmem,
        scratch_shapes=[
            pltpu.VMEM((total, depth_in), jnp.bfloat16),
            pltpu.VMEM((total, depth_out), jnp.bfloat16),
            pltpu.VMEM((depth_in, wide), jnp.bfloat16),
            pltpu.VMEM((depth_out, wide), jnp.bfloat16),
            pltpu.VMEM((outer, chunk, wide), jnp.float32),
            pltpu.VMEM((outer, inner - 1, chunk, wide), WIRE_X),
            pltpu.VMEM((outer, inner - 1, chunk, wide), WIRE_X),
            pltpu.VMEM((outer - 1, chunk, wide), WIRE_Z),
            pltpu.VMEM((outer - 1, chunk, wide), WIRE_Z),
            pltpu.VMEM((total, wide), jnp.bfloat16),
            dma((2, parts)),
            dma((outer, inner - 1)), dma((outer, inner - 1)),
            dma((outer - 1,)), dma((outer - 1,)),
            dma((outer - 1,)), dma((outer - 1,)),
            dma((outer, inner - 1)), dma((outer, inner - 1)),
        ],
        compiler_params=pltpu.CompilerParams(
            collective_id=0, has_side_effects=True, vmem_limit_bytes=58 * 1024 * 1024
        ),
    )(layer_inputs, output_grads, proj_in, proj_out)
    query = pl.pallas_call(
        sketch_kernel,
        out_shape=jax.ShapeDtypeStruct((examples, rank * rank), jnp.bfloat16),
        in_specs=[vmem, pl.BlockSpec(memory_space=pltpu.SMEM)],
        out_specs=vmem,
        scratch_shapes=[pltpu.VMEM((examples * rank, wide), jnp.float32)],
        compiler_params=pltpu.CompilerParams(vmem_limit_bytes=32 * 1024 * 1024),
    )(tokens, bounds)
    return pl.pallas_call(
        score_kernel,
        out_shape=jax.ShapeDtypeStruct((count, cores * examples), jnp.float32),
        in_specs=[vmem, vmem],
        out_specs=vmem,
        scratch_shapes=[pltpu.VMEM((cores * examples, rank * rank), jnp.bfloat16), dma, dma],
        compiler_params=pltpu.CompilerParams(
            collective_id=1, has_side_effects=True, vmem_limit_bytes=32 * 1024 * 1024
        ),
    )(moved, query)


def solution(mesh):
    placed = (
        P(("groups", "dp"), "tensor"),
        P(("groups", "dp"), "tensor"),
        P("tensor", None),
        P("tensor", None),
        P(),
        P(),
        P(("groups", "tensor", "dp"), None),
        P(("groups", "dp"), None),
    )
    return jax.shard_map(
        functools.partial(on_device, mesh.shape["tensor"], mesh.shape["dp"]),
        mesh=mesh,
        in_specs=placed,
        out_specs=P(("tensor", "dp"), "groups"),
        check_vma=False,
    )
```

time: 219 us -> 85.6 us (0.39)
  blocking collectives: 94.7 us -> 0 us
  Pallas kernels: 0 us -> 67.7 us
  matrix products: 55.4 us -> 6.45 us
  local copies, waits for them, and re-layouts: 36 us -> 10.9 us
  between operations: 13.5 us -> 0.1 us
  other arithmetic: 10.1 us -> 0.28 us
  waiting for transfers between devices: 7.77 us -> 0 us
    psum x1 -> x0, blocking collectives: 94.7 us -> none  [on_device(): lax.psum(project_rows(layer_inputs, output_grads, proj_in, proj_out), 'te...]
    pallas_call x0 -> x3, Pallas kernels: none -> 67.7 us  [the longest x1 57.5 us: on_device(): pl.pallas_call(functools.partial(token_kernel, outer, inner), out_shape=j...]
    dot_general x13 -> x2, matrix products: 55.4 us -> 6.45 us  [on_device(): jnp.einsum('ac,jab,db->jcd', inv_out, square, inv_in, precision=lax.Preci...]
    reshape x9 -> x1, local copies, waits for them, and re-layouts: 19.2 us -> 3.11 us  [on_device(): square = stored.astype(jnp.float32).reshape(count, rank, rank)]
    all_gather x1 -> x0, waiting for transfers between devices: 7.76 us -> none  [on_device(): lax.all_gather(query, 'dp', axis=0, tiled=True)]
    add x16 -> x0, other arithmetic: 7.68 us -> none  [the longest x8 5.06 us: segment_outer(): positions = first + lax.iota(jnp.int32, grad_rows.shape[0])]
    transpose x8 -> x0, local copies, waits for them, and re-layouts: 6.81 us -> none  [segment_outer(): grad_cols = grad_rows.T]
    dynamic_slice x8 -> x0, local copies, waits for them, and re-layouts: 5.2 us -> none  [blockwise_sketch(): lax.scan(step, initial, (grad_blocks, input_blocks, offsets))]
  transfers between devices with their start and end apart: 1 -> 0, of which waited for: 1 -> 0; matrix products, arithmetic and copies ran while one was open for 0% -> 0% of each run, Pallas kernels for 0% -> 0%
where the time goes in v1:
time: 85.6 us; the launch traced here: 85.3 us
  Pallas kernels  67.7 us (79%)
  local copies, waits for them, and re-layouts  10.9 us (13%)
  matrix products  6.45 us (8%)
    pallas_call x1, Pallas kernels, on_device(): pl.pallas_call(functools.partial(token_kernel, outer, inner), out_shape=j...  57.5 us
    pallas_call x1, Pallas kernels, on_device(): pl.pallas_call(sketch_kernel, out_shape=jax.ShapeDtypeStruct((examples, r...  7.71 us
    dot_general x2, matrix products, on_device(): jnp.einsum('ac,jab,db->jcd', inv_out, square, inv_in, precision=lax.Preci...  6.45 us
    unnamed x15, local copies, waits for them, and re-layouts  4.02 us
    dot_general x1, local copies, waits for them, and re-layouts, on_device(): jnp.einsum('ac,jab,db->jcd', inv_out, square, inv_in, precision=lax.Preci...  3.22 us
    reshape x1, local copies, waits for them, and re-layouts, on_device(): square = stored.astype(jnp.float32).reshape(count, rank, rank)  3.11 us
    pallas_call x1, Pallas kernels, on_device(): pl.pallas_call(score_kernel, out_shape=jax.ShapeDtypeStruct((count, cores...  2.45 us

profile of v1, /device:TPU:0, one launch (start us, length us, event | category | flops | bytes accessed | tf_op | source)
XLA Modules:
  0.0 85.3 jit_solution(17814948451583264600)
XLA Ops:
  0.0 0.0 copy-start
  0.0 3.1 %reshape.13 = bf16[80,64,64]{2,1,0:T(8,128)(2,1)} reshape(bf16[80,4096]{1,0:T(8,128)(2,1)} %param.14) | data formatting | bytes 1310720 | tf_op jit(solution)/shard_map/reshape | solution.py:235
  3.1 0.0 copy-done
  3.1 2.8 %fusion.1 = f32[80,64,64]{2,1,0:T(8,128)S(1)} fusion(bf16[80,64,64]{2,1,0:T(8,128)(2,1)} %reshape.13, f32[64,64]{1,0:T(8,128)S(1)} %copy-done), kind=kOutput, calls=%fused_computation.2 | convolution fusion | flops 251658240 | bytes 1982464 | tf_op jit(solution)/shard_map/ac,jab,db->jcd/dot_general | solution.py:236
  5.9 0.0 copy-start.4
  5.9 3.2 %copy.15 = f32[80,64,64]{0,1,2:T(8,128)} copy(f32[80,64,64]{2,1,0:T(8,128)S(1)} %fusion.1) | data formatting | bytes 2621440 | tf_op jit(solution)/shard_map/ac,jab,db->jcd/dot_general | solution.py:236
  9.2 0.0 copy-done.4
  9.2 0.0 copy-start.3
  9.2 0.0 copy-start.2
  9.2 3.7 %convolution_convert_fusion = bf16[80,64,64]{0,2,1:T(8,128)(2,1)S(1)} fusion(f32[80,64,64]{0,1,2:T(8,128)} %copy.15, f32[64,64]{1,0:T(8,128)S(1)} %copy-done.4), kind=kOutput, calls=%fused_computation | convolution fusion | flops 251985920 | bytes 1982464 | tf_op jit(solution)/shard_map/ac,jab,db->jcd/dot_general | solution.py:236
  12.8 0.5 copy.16.stored
  13.3 0.0 copy-done.3
  13.4 0.9 %copy.13.w_in = bf16[1024,64]{1,0:T(8,128)(2,1)} copy(bf16[1024,64]{0,1:T(8,128)(2,1)S(1)} %copy-done.3) | data formatting | bytes 262144 | tf_op args[2]
  14.2 0.0 copy-done.2
  14.2 1.3 %copy.14.w_out = bf16[3584,64]{1,0:T(8,128)(2,1)} copy(bf16[3584,64]{0,1:T(8,128)(2,1)S(1)} %copy-done.2) | data formatting | bytes 917504 | tf_op args[3]
  15.5 0.0 copy-start.5
  15.5 57.5 %shard_map.82.tokens = bf16[4096,128]{1,0:T(8,128)(2,1)} custom-call(bf16[4096,1024]{1,0:T(8,128)(2,1)} %x_hbm.1, bf16[4096,3584]{1,0:T(8,128)(2,1)} %g_hbm.1, bf16[1024,64]{1,0:T(8,128)(2,1)} %copy.13.w_in, bf16[3584,64]{1,0:T(8,128)(2,1)} %copy.14.w_out), custom_call_target="tpu_custom_call" | custom-call | tf_op jit(solution)/shard_map/pallas_call | solution.py:244
  73.0 0.0 copy-done.5
  73.0 0.2 reduce-window_clone.1
  73.3 0.0 copy-start.1
  73.3 1.2 %copy-done.1 = bf16[4096,128]{1,0:T(8,128)(2,1)S(1)} copy-done((bf16[4096,128]{1,0:T(8,128)(2,1)S(1)}, bf16[4096,128]{1,0:T(8,128)(2,1)}, u32[]{:S(2)}) %copy-start.1) | copy-done | bytes 1048600
  74.5 7.7 %shard_map.83.query = bf16[64,4096]{1,0:T(8,128)(2,1)S(1)} custom-call(bf16[4096,128]{1,0:T(8,128)(2,1)S(1)} %copy-done.1, s32[3,64]{1,0:T(4,128)S(1)} %pad_add_fusion.bounds), custom_call_target="tpu_custom_call" | custom-call | tf_op jit(solution)/shard_map/pallas_call | solution.py:270
  82.3 2.5 %shard_map.84 = f32[80,128]{1,0:T(8,128)S(1)} custom-call(bf16[80,4096]{1,0:T(8,128)(2,1)S(1)} %copy.16.stored, bf16[64,4096]{1,0:T(8,128)(2,1)S(1)} %shard_map.83.query), custom_call_target="tpu_custom_call" | custom-call | tf_op jit(solution)/shard_map/pallas_call | solution.py:278
  84.7 0.6 copy.18
  (3 shorter events, 0.0 us)
Async XLA Ops:
  0.0 3.1 %copy-start = (f32[64,64]{1,0:T(8,128)S(1)}, f32[64,64]{1,0:T(8,128)}, u32[]{:S(2)}) copy-start(f32[64,64]{1,0:T(8,128)} %param.12) | copy-start | bytes 49156
  5.9 3.2 %copy-start.4 = (f32[64,64]{1,0:T(8,128)S(1)}, f32[64,64]{1,0:T(8,128)}, u32[]{:S(2)}) copy-start(f32[64,64]{1,0:T(8,128)} %param.13) | copy-start | bytes 49156
  9.2 4.2 %copy-start.3 = (bf16[1024,64]{0,1:T(8,128)(2,1)S(1)}, bf16[1024,64]{0,1:T(8,128)(2,1)}, u32[]{:S(2)}) copy-start(bf16[1024,64]{0,1:T(8,128)(2,1)} %param.10) | copy-start | bytes 393220
  9.2 5.1 %copy-start.2 = (bf16[3584,64]{0,1:T(8,128)(2,1)S(1)}, bf16[3584,64]{0,1:T(8,128)(2,1)}, u32[]{:S(2)}) copy-start(bf16[3584,64]{0,1:T(8,128)(2,1)} %param.11) | copy-start | bytes 1376260
  15.5 57.5 %copy-start.5 = (s32[1,64]{1,0:T(1,128)S(1)}, s32[1,64]{1,0:T(1,128)}, u32[]{:S(2)}) copy-start(s32[1,64]{1,0:T(1,128)} %param.15) | copy-start | bytes 772
  73.3 1.2 %copy-start.1 = (bf16[4096,128]{1,0:T(8,128)(2,1)S(1)}, bf16[4096,128]{1,0:T(8,128)(2,1)}, u32[]{:S(2)}) copy-start(bf16[4096,128]{1,0:T(8,128)(2,1)} %shard_map.82.tokens) | copy-start | bytes 3145732

commit v2 on v1

--- a/solution.py
+++ b/solution.py
@@ -25,18 +25,69 @@
     return inner
 
 
+def across(left, right):
+    return lax.dot_general(left, right, (((1,), (1,)), ((), ())), preferred_element_type=jnp.float32)
+
+
+def split(value):
+    high = value.astype(jnp.bfloat16)
+    return high, (value - high.astype(jnp.float32)).astype(jnp.bfloat16)
+
+
+def move_preconditioner(stored, inv_out, inv_in, mixed, moved):
+    count = stored.shape[0]
+    rank = inv_in.shape[0]
+    wide = 2 * rank
+    high, low = split(inv_in[...])
+    high = jnp.concatenate([high, high], axis=1)
+    low = jnp.concatenate([low, low], axis=1)
+    none = jnp.zeros_like(high)
+    first = jnp.concatenate([high, none, low, none], axis=0)
+    second = jnp.concatenate([none, high, none, low], axis=0)
+    for a in range(0, rank, 2):
+        pair = stored[:, a * rank:(a + 2) * rank]
+        pair = jnp.concatenate([pair, pair], axis=1)
+        mixed[pl.ds(a, count, stride=rank), :] = jnp.dot(
+            pair, first, preferred_element_type=jnp.float32
+        )
+        mixed[pl.ds(a + 1, count, stride=rank), :] = jnp.dot(
+            pair, second, preferred_element_type=jnp.float32
+        )
+    out_high, out_low = split(inv_out[...])
+    factor = jnp.concatenate([out_high, out_low, out_high], axis=1)
+
+    def one(j, carry):
+        rows = pl.ds(pl.multiple_of(j * rank, rank), rank)
+        row_high, row_low = split(mixed[rows, :])
+        mixed[rows, :] = jnp.dot(
+            factor,
+            jnp.concatenate([row_high, row_high, row_low], axis=0),
+            preferred_element_type=jnp.float32,
+        )
+        return carry
+
+    lax.fori_loop(0, count, one, 0, unroll=4)
+    left = lax.broadcasted_iota(jnp.int32, (count, wide), 1) < rank
+    for a in range(0, rank, 2):
+        moved[:, a * rank:(a + 2) * rank] = jnp.where(
+            left,
+            mixed[pl.ds(a, count, stride=rank), :],
+            mixed[pl.ds(a + 1, count, stride=rank), :],
+        ).astype(moved.dtype)
+
+
 def token_kernel(
     outer, inner,
-    x_hbm, g_hbm, w_in, w_out,
-    tokens_out,
+    x_hbm, g_hbm, w_in, w_out, stored, inv_out, inv_in,
+    tokens_out, moved_out,
     x_buf, g_buf, w_x, w_g, own, send_x, recv_x, send_z, recv_z,
-    tokens,
+    tokens, mixed,
     load_sem, sx_sem, rx_sem, sz_sem, rz_sem, gz_send, gz_recv, gx_send, gx_recv,
 ):
     parts = outer * inner
     total = x_buf.shape[0]
     chunk = total // parts
-    rank = w_in.shape[1]
+    rank = w_in.shape[0]
     wide = 2 * rank
     me = lax.axis_index("tensor")
     my_o = me // inner
@@ -69,8 +120,8 @@
     for peer in peers:
         pl.semaphore_signal(barrier, inc=1, device_id=peer, device_id_type=MESH)
 
-    w_x[...] = jnp.concatenate([w_in[...], jnp.zeros_like(w_in)], axis=1)
-    w_g[...] = jnp.concatenate([jnp.zeros_like(w_out), w_out[...]], axis=1)
+    w_x[...] = jnp.concatenate([w_in[...], jnp.zeros_like(w_in)], axis=0)
+    w_g[...] = jnp.concatenate([jnp.zeros_like(w_out), w_out[...]], axis=0)
     pl.semaphore_wait(barrier, len(peers))
 
     sub = min(256, chunk)
@@ -87,8 +138,8 @@
         @pl.loop(0, chunk // sub)
         def _(h):
             rows = pl.ds(pl.multiple_of(base + h * sub, sub), sub)
-            value = jnp.dot(x_buf[rows, :], w_x[...], preferred_element_type=jnp.float32)
-            value += jnp.dot(g_buf[rows, :], w_g[...], preferred_element_type=jnp.float32)
+            value = across(x_buf[rows, :], w_x[...])
+            value += across(g_buf[rows, :], w_g[...])
             dest[pl.ds(pl.multiple_of(h * sub, sub), sub), :] = value.astype(dest.dtype)
 
     def x_copy(s, r):
@@ -129,6 +180,8 @@
             if s >= LAG:
                 combine(s - LAG)
     for s in range(outer - min(LAG, outer), outer):
+        if s == outer - 1:
+            move_preconditioner(stored, inv_out, inv_in, mixed, moved_out)
         combine(s)
 
     def gather_z(s):
@@ -169,28 +222,29 @@
     tokens_out[...] = tokens[...]
 
 
-def sketch_kernel(tokens, bounds, query, sketch):
+def sketch_kernel(tokens, lengths, query, sketch):
     total, wide = tokens.shape
     rank = wide // 2
-    examples = bounds.shape[1]
+    examples = lengths.shape[1]
     window = window_of(total)
     row = lax.broadcasted_iota(jnp.int32, (window, wide), 0)
     left = lax.broadcasted_iota(jnp.int32, (window, wide), 1) < rank
 
-    def example(e, carry):
-        first = pl.multiple_of(bounds[0, e], 16)
+    def example(e, begin):
+        finish = begin + lengths[0, e]
+        first = pl.multiple_of(jnp.minimum((begin // 16) * 16, total - window), 16)
         rows = tokens[pl.ds(first, window), :]
         wide_rows = rows.astype(jnp.float32)
         twice = jnp.where(left, wide_rows, pltpu.roll(wide_rows, rank, 1))
-        inside = (row >= bounds[1, e]) & (row < bounds[2, e])
+        inside = (row >= begin - first) & (row < finish - first)
         picked = jnp.where(inside, twice, 0.0).astype(jnp.bfloat16)
         outer_product = lax.dot_general(
             rows, picked, (((0,), (0,)), ((), ())), preferred_element_type=jnp.float32
         )
         sketch[pl.ds(pl.multiple_of(e * rank, rank), rank), :] = outer_product[rank:, :]
-        return carry
-
-    lax.fori_loop(0, examples, example, 0, unroll=4)
+        return finish
+
+    lax.fori_loop(0, examples, example, jnp.int32(0), unroll=8)
 
     low = lax.broadcasted_iota(jnp.int32, (examples, wide), 1) < rank
     for a in range(0, rank, 2):
@@ -232,31 +286,28 @@
     chunk = total // parts
     examples = lengths.shape[1]
     count = stored.shape[0]
-    square = stored.astype(jnp.float32).reshape(count, rank, rank)
-    moved = jnp.einsum("ac,jab,db->jcd", inv_out, square, inv_in, precision=lax.Precision.HIGHEST)
-    moved = moved.reshape(count, rank * rank).astype(jnp.bfloat16)
-    ends = jnp.cumsum(lengths[0])
-    begins = ends - lengths[0]
-    firsts = jnp.minimum((begins // 16) * 16, total - window_of(total))
-    bounds = jnp.stack([firsts, begins - firsts, ends - firsts])
     vmem = pl.BlockSpec(memory_space=pltpu.VMEM)
     dma = pltpu.SemaphoreType.DMA
-    tokens = pl.pallas_call(
+    tokens, moved = pl.pallas_call(
         functools.partial(token_kernel, outer, inner),
-        out_shape=jax.ShapeDtypeStruct((total, wide), jnp.bfloat16),
-        in_specs=[pl.BlockSpec(memory_space=pl.ANY), pl.BlockSpec(memory_space=pl.ANY), vmem, vmem],
-        out_specs=vmem,
+        out_shape=(
+            jax.ShapeDtypeStruct((total, wide), jnp.bfloat16),
+            jax.ShapeDtypeStruct((count, rank * rank), jnp.bfloat16),
+        ),
+        in_specs=[pl.BlockSpec(memory_space=pl.ANY), pl.BlockSpec(memory_space=pl.ANY)] + [vmem] * 5,
+        out_specs=(vmem, vmem),
         scratch_shapes=[
             pltpu.VMEM((total, depth_in), jnp.bfloat16),
             pltpu.VMEM((total, depth_out), jnp.bfloat16),
-            pltpu.VMEM((depth_in, wide), jnp.bfloat16),
-            pltpu.VMEM((depth_out, wide), jnp.bfloat16),
+            pltpu.VMEM((wide, depth_in), jnp.bfloat16),
+            pltpu.VMEM((wide, depth_out), jnp.bfloat16),
             pltpu.VMEM((outer, chunk, wide), jnp.float32),
             pltpu.VMEM((outer, inner - 1, chunk, wide), WIRE_X),
             pltpu.VMEM((outer, inner - 1, chunk, wide), WIRE_X),
             pltpu.VMEM((outer - 1, chunk, wide), WIRE_Z),
             pltpu.VMEM((outer - 1, chunk, wide), WIRE_Z),
             pltpu.VMEM((total, wide), jnp.bfloat16),
+            pltpu.VMEM((count * rank, wide), jnp.float32),
             dma((2, parts)),
             dma((outer, inner - 1)), dma((outer, inner - 1)),
             dma((outer - 1,)), dma((outer - 1,)),
@@ -266,7 +317,7 @@
         compiler_params=pltpu.CompilerParams(
             collective_id=0, has_side_effects=True, vmem_limit_bytes=58 * 1024 * 1024
         ),
-    )(layer_inputs, output_grads, proj_in, proj_out)
+    )(layer_inputs, output_grads, proj_in.T, proj_out.T, stored, inv_out, inv_in)
     query = pl.pallas_call(
         sketch_kernel,
         out_shape=jax.ShapeDtypeStruct((examples, rank * rank), jnp.bfloat16),
@@ -274,7 +325,7 @@
         out_specs=vmem,
         scratch_shapes=[pltpu.VMEM((examples * rank, wide), jnp.float32)],
         compiler_params=pltpu.CompilerParams(vmem_limit_bytes=32 * 1024 * 1024),
-    )(tokens, bounds)
+    )(tokens, lengths)
     return pl.pallas_call(
         score_kernel,
         out_shape=jax.ShapeDtypeStruct((count, cores * examples), jnp.float32),

time: 85.6 us -> 69.5 us (0.81)
  local copies, waits for them, and re-layouts: 10.9 us -> 2.92 us
  matrix products: 6.45 us -> 0 us
  Pallas kernels: 67.7 us -> 66.3 us
    dot_general x2 -> x0, matrix products: 6.45 us -> none  [on_device(): jnp.einsum('ac,jab,db->jcd', inv_out, square, inv_in, precision=lax.Preci...]
    dot_general x1 -> x0, local copies, waits for them, and re-layouts: 3.22 us -> none  [on_device(): jnp.einsum('ac,jab,db->jcd', inv_out, square, inv_in, precision=lax.Preci...]
    reshape x1 -> x0, local copies, waits for them, and re-layouts: 3.11 us -> none  [on_device(): square = stored.astype(jnp.float32).reshape(count, rank, rank)]
    pallas_call x1, Pallas kernels: 7.71 us -> 6.13 us  [on_device(): pl.pallas_call(sketch_kernel, out_shape=jax.ShapeDtypeStruct((examples, r...]
    unnamed x15 -> x7, local copies, waits for them, and re-layouts: 4.02 us -> 2.92 us
where the time goes in v2:
time: 69.5 us; the launch traced here: 69.3 us
  Pallas kernels  66.3 us (95%)
  local copies, waits for them, and re-layouts  2.92 us (4%)
    pallas_call x1, Pallas kernels, on_device(): pl.pallas_call(functools.partial(token_kernel, outer, inner), out_shape=(...  57.8 us
    pallas_call x1, Pallas kernels, on_device(): pl.pallas_call(sketch_kernel, out_shape=jax.ShapeDtypeStruct((examples, r...  6.13 us
    unnamed x7, local copies, waits for them, and re-layouts  2.92 us
    pallas_call x1, Pallas kernels, on_device(): pl.pallas_call(score_kernel, out_shape=jax.ShapeDtypeStruct((count, cores...  2.41 us

profile of v2, /device:TPU:0, one launch (start us, length us, event | category | flops | bytes accessed | tf_op | source)
XLA Modules:
  0.0 69.3 jit_solution(9837534921764193936)
XLA Ops:
  0.0 0.0 copy-start.2
  0.0 57.8 %shard_map.82 = (bf16[4096,128]{1,0:T(8,128)(2,1)}, bf16[80,4096]{1,0:T(8,128)(2,1)}) custom-call(bf16[4096,1024]{1,0:T(8,128)(2,1)} %x_hbm.1, bf16[4096,3584]{1,0:T(8,128)(2,1)} %g_hbm.1, bf16[64,1024]{1,0:T(8,128)(2,1)} %bitcast.3, bf16[64,3584]{1,0:T(8,128)(2,1)} %bitcast.2, bf16[80,4096]{1,0:T(8,128)(2,1)} %stored.1, f32[64,64]{1,0:T(8,128)} %inv_out.1, ...), custom_call_target="tpu_custom_call" | custom-call | tf_op jit(solution)/shard_map/pallas_call | solution.py:291
  57.8 0.0 copy-done.2
  57.8 0.0 copy-start
  57.8 1.2 %copy-done = bf16[4096,128]{1,0:T(8,128)(2,1)S(1)} copy-done((bf16[4096,128]{1,0:T(8,128)(2,1)S(1)}, bf16[4096,128]{1,0:T(8,128)(2,1)}, u32[]{:S(2)}) %copy-start) | copy-done | bytes 1048600
  59.0 6.1 %shard_map.83.query = bf16[64,4096]{1,0:T(8,128)(2,1)S(1)} custom-call(bf16[4096,128]{1,0:T(8,128)(2,1)S(1)} %copy-done, s32[1,64]{1,0:T(1,128)S(1)} %copy-done.2), custom_call_target="tpu_custom_call" | custom-call | tf_op jit(solution)/shard_map/pallas_call | solution.py:321
  65.2 0.0 copy-start.1
  65.2 1.1 %copy-done.1 = bf16[80,4096]{1,0:T(8,128)(2,1)S(1)} copy-done((bf16[80,4096]{1,0:T(8,128)(2,1)S(1)}, bf16[80,4096]{1,0:T(8,128)(2,1)}, u32[]{:S(2)}) %copy-start.1) | copy-done | bytes 655384
  66.3 2.4 %shard_map.84 = f32[80,128]{1,0:T(8,128)S(1)} custom-call(bf16[80,4096]{1,0:T(8,128)(2,1)S(1)} %copy-done.1, bf16[64,4096]{1,0:T(8,128)(2,1)S(1)} %shard_map.83.query), custom_call_target="tpu_custom_call" | custom-call | tf_op jit(solution)/shard_map/pallas_call | solution.py:329
  68.7 0.6 copy.10
Async XLA Ops:
  0.0 57.8 %copy-start.2 = (s32[1,64]{1,0:T(1,128)S(1)}, s32[1,64]{1,0:T(1,128)}, u32[]{:S(2)}) copy-start(s32[1,64]{1,0:T(1,128)} %lengths.1) | copy-start | bytes 772
  57.8 1.2 %copy-start = (bf16[4096,128]{1,0:T(8,128)(2,1)S(1)}, bf16[4096,128]{1,0:T(8,128)(2,1)}, u32[]{:S(2)}) copy-start(bf16[4096,128]{1,0:T(8,128)(2,1)} %get-tuple-element.8.tokens) | copy-start | bytes 3145732
  65.2 1.1 %copy-start.1 = (bf16[80,4096]{1,0:T(8,128)(2,1)S(1)}, bf16[80,4096]{1,0:T(8,128)(2,1)}, u32[]{:S(2)}) copy-start(bf16[80,4096]{1,0:T(8,128)(2,1)} %get-tuple-element.7.stored) | copy-start | bytes 1966084

commit v3 on v2

--- a/solution.py
+++ b/solution.py
@@ -8,8 +8,6 @@
 
 MESH = pl.DeviceIdType.MESH
 LONGEST = 128
-WIRE_X = jnp.float32
-WIRE_Z = jnp.float32
 AHEAD = 3
 LAG = 1
 
@@ -23,6 +21,15 @@
     while (2 * inner) ** 3 <= count:
         inner *= 2
     return inner
+
+
+def flip(place, bits):
+    result, bit = place, 1
+    while bit <= bits:
+        if bits & bit:
+            result = result + bit - 2 * bit * ((place // bit) % 2)
+        bit *= 2
+    return result
 
 
 def across(left, right):
@@ -69,18 +76,19 @@
     lax.fori_loop(0, count, one, 0, unroll=4)
     left = lax.broadcasted_iota(jnp.int32, (count, wide), 1) < rank
     for a in range(0, rank, 2):
-        moved[:, a * rank:(a + 2) * rank] = jnp.where(
+        pair = jnp.where(
             left,
             mixed[pl.ds(a, count, stride=rank), :],
             mixed[pl.ds(a + 1, count, stride=rank), :],
-        ).astype(moved.dtype)
+        )
+        moved[:count, a * rank:(a + 2) * rank], moved[count:, a * rank:(a + 2) * rank] = split(pair)
 
 
 def token_kernel(
     outer, inner,
     x_hbm, g_hbm, w_in, w_out, stored, inv_out, inv_in,
     tokens_out, moved_out,
-    x_buf, g_buf, w_x, w_g, own, send_x, recv_x, send_z, recv_z,
+    x_buf, g_buf, w_x, w_g, own, send_x, recv_x, send_far, recv_far, send_near, recv_near,
     tokens, mixed,
     load_sem, sx_sem, rx_sem, sz_sem, rz_sem, gz_send, gz_recv, gx_send, gx_recv,
 ):
@@ -98,7 +106,7 @@
 
     order = []
     for s in range(outer):
-        o = lax.rem(my_o + 1 + s, outer)
+        o = flip(my_o, outer - 1 - s)
         for r in list(range(1, inner)) + [0]:
             order.append((s, r, o, lax.rem(my_i + r, inner)))
 
@@ -115,7 +123,7 @@
             copy.start()
 
     barrier = pltpu.get_barrier_semaphore()
-    peers = [{"tensor": lax.rem(my_o + s, outer) * inner + my_i} for s in range(1, outer)]
+    peers = [{"tensor": flip(my_o, s) * inner + my_i} for s in range(1, outer)]
     peers += [{"tensor": my_o * inner + lax.rem(my_i + r, inner)} for r in range(1, inner)]
     for peer in peers:
         pl.semaphore_signal(barrier, inc=1, device_id=peer, device_id_type=MESH)
@@ -149,11 +157,17 @@
             device_id={"tensor": my_o * inner + lax.rem(my_i + r, inner)}, device_id_type=MESH,
         )
 
+    def send_z(s):
+        return send_near if s == outer - 2 else send_far.at[s]
+
+    def recv_z(s):
+        return recv_near if s == outer - 2 else recv_far.at[s]
+
     def z_copy(s):
         return pltpu.make_async_remote_copy(
-            src_ref=send_z.at[s], dst_ref=recv_z.at[s],
+            src_ref=send_z(s), dst_ref=recv_z(s),
             send_sem=sz_sem.at[s], recv_sem=rz_sem.at[s],
-            device_id={"tensor": lax.rem(my_o + 1 + s, outer) * inner + my_i}, device_id_type=MESH,
+            device_id={"tensor": flip(my_o, outer - 1 - s) * inner + my_i}, device_id_type=MESH,
         )
 
     def combine(s):
@@ -162,12 +176,13 @@
             x_copy(s, r).wait_recv()
             value = value + recv_x[s, r - 1].astype(jnp.float32)
         if s < outer - 1:
-            send_z[s] = value.astype(send_z.dtype)
+            target = send_z(s)
+            target[...] = value.astype(target.dtype)
             z_copy(s).start()
         else:
             for q in range(outer - 1):
                 z_copy(q).wait_recv()
-                value = value + recv_z[q].astype(jnp.float32)
+                value = value + recv_z(q)[...].astype(jnp.float32)
             tokens[rows_of(my_o, my_i), :] = value.astype(tokens.dtype)
 
     for k in range(parts):
@@ -189,11 +204,11 @@
         return pltpu.make_async_remote_copy(
             src_ref=tokens.at[rows], dst_ref=tokens.at[rows],
             send_sem=gz_send.at[s], recv_sem=gz_recv.at[s],
-            device_id={"tensor": lax.rem(my_o + 1 + s, outer) * inner + my_i}, device_id_type=MESH,
+            device_id={"tensor": flip(my_o, outer - 1 - s) * inner + my_i}, device_id_type=MESH,
         )
 
     def gather_x(s, r):
-        rows = rows_of(lax.rem(my_o + outer - s, outer), my_i)
+        rows = rows_of(flip(my_o, outer - s) if s else my_o, my_i)
         return pltpu.make_async_remote_copy(
             src_ref=tokens.at[rows], dst_ref=tokens.at[rows],
             send_sem=gx_send.at[s, r - 1], recv_sem=gx_recv.at[s, r - 1],
@@ -253,15 +268,17 @@
             sketch[pl.ds(a, examples, stride=rank), :],
             sketch[pl.ds(a + 1, examples, stride=rank), :],
         )
-        query[:, a * rank:(a + 2) * rank] = pair.astype(query.dtype)
+        columns = slice(a * rank, (a + 2) * rank)
+        query[:examples, columns], query[examples:, columns] = split(pair)
 
 
 def score_kernel(stored, query, out, both, pair_send, pair_recv):
     core = lax.axis_index("dp")
-    examples = query.shape[0]
+    examples = query.shape[0] // 2
+    count = stored.shape[0] // 2
     barrier = pltpu.get_barrier_semaphore()
     pl.semaphore_signal(barrier, inc=1, device_id={"dp": 1 - core}, device_id_type=MESH)
-    mine = pl.ds(pl.multiple_of(core * examples, examples), examples)
+    mine = pl.ds(pl.multiple_of(core * 2 * examples, 2 * examples), 2 * examples)
     both[mine, :] = query[...]
     pl.semaphore_wait(barrier, 1)
     swap = pltpu.make_async_remote_copy(
@@ -271,9 +288,13 @@
     )
     swap.start()
     swap.wait()
-    out[...] = lax.dot_general(
-        stored[...], both[...], (((1,), (1,)), ((), ())), preferred_element_type=jnp.float32
-    )
+    product = across(stored[...], both[...])
+    halves = []
+    for other in range(both.shape[0] // (2 * examples)):
+        at = other * 2 * examples
+        high = product[:, at:at + examples]
+        halves.append(high[:count] + high[count:] + product[:count, at + examples:at + 2 * examples])
+    out[...] = jnp.concatenate(halves, axis=1)
 
 
 def on_device(parts, cores, layer_inputs, output_grads, proj_in, proj_out, inv_out, inv_in, stored, lengths):
@@ -286,13 +307,14 @@
     chunk = total // parts
     examples = lengths.shape[1]
     count = stored.shape[0]
+    wire = jnp.bfloat16 if parts <= 8 else jnp.float32
     vmem = pl.BlockSpec(memory_space=pltpu.VMEM)
     dma = pltpu.SemaphoreType.DMA
     tokens, moved = pl.pallas_call(
         functools.partial(token_kernel, outer, inner),
         out_shape=(
             jax.ShapeDtypeStruct((total, wide), jnp.bfloat16),
-            jax.ShapeDtypeStruct((count, rank * rank), jnp.bfloat16),
+            jax.ShapeDtypeStruct((2 * count, rank * rank), jnp.bfloat16),
         ),
         in_specs=[pl.BlockSpec(memory_space=pl.ANY), pl.BlockSpec(memory_space=pl.ANY)] + [vmem] * 5,
         out_specs=(vmem, vmem),
@@ -302,10 +324,12 @@
             pltpu.VMEM((wide, depth_in), jnp.bfloat16),
             pltpu.VMEM((wide, depth_out), jnp.bfloat16),
             pltpu.VMEM((outer, chunk, wide), jnp.float32),
-            pltpu.VMEM((outer, inner - 1, chunk, wide), WIRE_X),
-            pltpu.VMEM((outer, inner - 1, chunk, wide), WIRE_X),
-            pltpu.VMEM((outer - 1, chunk, wide), WIRE_Z),
-            pltpu.VMEM((outer - 1, chunk, wide), WIRE_Z),
+            pltpu.VMEM((outer, inner - 1, chunk, wide), wire),
+            pltpu.VMEM((outer, inner - 1, chunk, wide), wire),
+            pltpu.VMEM((max(outer - 2, 1), chunk, wide), wire),
+            pltpu.VMEM((max(outer - 2, 1), chunk, wide), wire),
+            pltpu.VMEM((chunk, wide), jnp.float32),
+            pltpu.VMEM((chunk, wide), jnp.float32),
             pltpu.VMEM((total, wide), jnp.bfloat16),
             pltpu.VMEM((count * rank, wide), jnp.float32),
             dma((2, parts)),
@@ -320,7 +344,7 @@
     )(layer_inputs, output_grads, proj_in.T, proj_out.T, stored, inv_out, inv_in)
     query = pl.pallas_call(
         sketch_kernel,
-        out_shape=jax.ShapeDtypeStruct((examples, rank * rank), jnp.bfloat16),
+        out_shape=jax.ShapeDtypeStruct((2 * examples, rank * rank), jnp.bfloat16),
         in_specs=[vmem, pl.BlockSpec(memory_space=pltpu.SMEM)],
         out_specs=vmem,
         scratch_shapes=[pltpu.VMEM((examples * rank, wide), jnp.float32)],
@@ -331,7 +355,7 @@
         out_shape=jax.ShapeDtypeStruct((count, cores * examples), jnp.float32),
         in_specs=[vmem, vmem],
         out_specs=vmem,
-        scratch_shapes=[pltpu.VMEM((cores * examples, rank * rank), jnp.bfloat16), dma, dma],
+        scratch_shapes=[pltpu.VMEM((2 * cores * examples, rank * rank), jnp.bfloat16), dma, dma],
         compiler_params=pltpu.CompilerParams(
             collective_id=1, has_side_effects=True, vmem_limit_bytes=32 * 1024 * 1024
         ),

time: 69.5 us -> 62.1 us (0.89)
  Pallas kernels: 66.3 us -> 58.7 us
    pallas_call x1, Pallas kernels: 57.8 us -> 48.8 us  [on_device(): pl.pallas_call(functools.partial(token_kernel, outer, inner), out_shape=(...]
    pallas_call x1, Pallas kernels: 2.41 us -> 3.63 us  [on_device(): pl.pallas_call(score_kernel, out_shape=jax.ShapeDtypeStruct((count, cores...]
where the time goes in v3:
time: 62.1 us; the launch traced here: 61.9 us
  Pallas kernels  58.7 us (95%)
  local copies, waits for them, and re-layouts  3.15 us (5%)
    pallas_call x1, Pallas kernels, on_device(): pl.pallas_call(functools.partial(token_kernel, outer, inner), out_shape=(...  48.8 us
    pallas_call x1, Pallas kernels, on_device(): pl.pallas_call(sketch_kernel, out_shape=jax.ShapeDtypeStruct((2 * example...  6.2 us
    pallas_call x1, Pallas kernels, on_device(): pl.pallas_call(score_kernel, out_shape=jax.ShapeDtypeStruct((count, cores...  3.63 us
    unnamed x7, local copies, waits for them, and re-layouts  3.15 us

profile of v3, /device:TPU:0, one launch (start us, length us, event | category | flops | bytes accessed | tf_op | source)
XLA Modules:
  0.0 61.9 jit_solution(4862512990188871313)
XLA Ops:
  0.0 0.0 copy-start.2
  0.0 48.8 %shard_map.82 = (bf16[4096,128]{1,0:T(8,128)(2,1)}, bf16[160,4096]{1,0:T(8,128)(2,1)}) custom-call(bf16[4096,1024]{1,0:T(8,128)(2,1)} %x_hbm.1, bf16[4096,3584]{1,0:T(8,128)(2,1)} %g_hbm.1, bf16[64,1024]{1,0:T(8,128)(2,1)} %bitcast.3, bf16[64,3584]{1,0:T(8,128)(2,1)} %bitcast.2, bf16[80,4096]{1,0:T(8,128)(2,1)} %stored.1, f32[64,64]{1,0:T(8,128)} %inv_out.1, ...), custom_call_target="tpu_custom_call" | custom-call | tf_op jit(solution)/shard_map/pallas_call | solution.py:313
  48.9 0.0 copy-done.2
  48.9 0.0 copy-start.1
  48.9 1.2 %copy-done.1 = bf16[4096,128]{1,0:T(8,128)(2,1)S(1)} copy-done((bf16[4096,128]{1,0:T(8,128)(2,1)S(1)}, bf16[4096,128]{1,0:T(8,128)(2,1)}, u32[]{:S(2)}) %copy-start.1) | copy-done | bytes 1048600
  50.1 6.2 %shard_map.83.query = bf16[128,4096]{1,0:T(8,128)(2,1)S(1)} custom-call(bf16[4096,128]{1,0:T(8,128)(2,1)S(1)} %copy-done.1, s32[1,64]{1,0:T(1,128)S(1)} %copy-done.2), custom_call_target="tpu_custom_call" | custom-call | tf_op jit(solution)/shard_map/pallas_call | solution.py:345
  56.3 0.0 copy-start
  56.3 1.3 %copy-done = bf16[160,4096]{1,0:T(8,128)(2,1)S(1)} copy-done((bf16[160,4096]{1,0:T(8,128)(2,1)S(1)}, bf16[160,4096]{1,0:T(8,128)(2,1)}, u32[]{:S(2)}) %copy-start) | copy-done | bytes 1310744
  57.6 3.6 %shard_map.84 = f32[80,128]{1,0:T(8,128)S(1)} custom-call(bf16[160,4096]{1,0:T(8,128)(2,1)S(1)} %copy-done, bf16[128,4096]{1,0:T(8,128)(2,1)S(1)} %shard_map.83.query), custom_call_target="tpu_custom_call" | custom-call | tf_op jit(solution)/shard_map/pallas_call | solution.py:353
  61.3 0.6 %copy.10 = f32[80,128]{1,0:T(8,128)} copy(f32[80,128]{1,0:T(8,128)S(1)} %shard_map.84) | data formatting | bytes 81920
Async XLA Ops:
  0.0 48.9 %copy-start.2 = (s32[1,64]{1,0:T(1,128)S(1)}, s32[1,64]{1,0:T(1,128)}, u32[]{:S(2)}) copy-start(s32[1,64]{1,0:T(1,128)} %lengths.1) | copy-start | bytes 772
  48.9 1.2 %copy-start.1 = (bf16[4096,128]{1,0:T(8,128)(2,1)S(1)}, bf16[4096,128]{1,0:T(8,128)(2,1)}, u32[]{:S(2)}) copy-start(bf16[4096,128]{1,0:T(8,128)(2,1)} %get-tuple-element.8.tokens) | copy-start | bytes 3145732
  56.3 1.3 %copy-start = (bf16[160,4096]{1,0:T(8,128)(2,1)S(1)}, bf16[160,4096]{1,0:T(8,128)(2,1)}, u32[]{:S(2)}) copy-start(bf16[160,4096]{1,0:T(8,128)(2,1)} %get-tuple-element.7.stored) | copy-start | bytes 3932164

commit v4 on v3

--- a/solution.py
+++ b/solution.py
@@ -195,8 +195,6 @@
             if s >= LAG:
                 combine(s - LAG)
     for s in range(outer - min(LAG, outer), outer):
-        if s == outer - 1:
-            move_preconditioner(stored, inv_out, inv_in, mixed, moved_out)
         combine(s)
 
     def gather_z(s):
@@ -215,14 +213,15 @@
             device_id={"tensor": my_o * inner + lax.rem(my_i + r, inner)}, device_id_type=MESH,
         )
 
-    for s in range(outer - 1):
+    for s in reversed(range(outer - 1)):
         gather_z(s).start()
     for r in range(1, inner):
         gather_x(0, r).start()
-    for s in range(outer - 1):
+    for s in reversed(range(outer - 1)):
         gather_z(s).wait_recv()
         for r in range(1, inner):
             gather_x(s + 1, r).start()
+    move_preconditioner(stored, inv_out, inv_in, mixed, moved_out)
     for s in range(outer):
         for r in range(1, inner):
             gather_x(s, r).wait_recv()

time: 62.1 us -> 63.3 us (1.019)
  Pallas kernels: 58.7 us -> 59.9 us
    pallas_call x1, Pallas kernels: 48.8 us -> 50.1 us  [on_device(): pl.pallas_call(functools.partial(token_kernel, outer, inner), out_shape=(...]
where the time goes in v4:
time: 63.3 us; the launch traced here: 63.1 us
  Pallas kernels  59.9 us (95%)
  local copies, waits for them, and re-layouts  3.15 us (5%)
    pallas_call x1, Pallas kernels, on_device(): pl.pallas_call(functools.partial(token_kernel, outer, inner), out_shape=(...  50.1 us
    pallas_call x1, Pallas kernels, on_device(): pl.pallas_call(sketch_kernel, out_shape=jax.ShapeDtypeStruct((2 * example...  6.2 us
    pallas_call x1, Pallas kernels, on_device(): pl.pallas_call(score_kernel, out_shape=jax.ShapeDtypeStruct((count, cores...  3.63 us
    unnamed x7, local copies, waits for them, and re-layouts  3.15 us

profile of v4, /device:TPU:0, one launch (start us, length us, event | category | flops | bytes accessed | tf_op | source)
XLA Modules:
  0.0 63.1 jit_solution(1792099482457207568)
XLA Ops:
  0.0 0.0 copy-start.2
  0.0 50.1 %shard_map.82 = (bf16[4096,128]{1,0:T(8,128)(2,1)}, bf16[160,4096]{1,0:T(8,128)(2,1)}) custom-call(bf16[4096,1024]{1,0:T(8,128)(2,1)} %x_hbm.1, bf16[4096,3584]{1,0:T(8,128)(2,1)} %g_hbm.1, bf16[64,1024]{1,0:T(8,128)(2,1)} %bitcast.3, bf16[64,3584]{1,0:T(8,128)(2,1)} %bitcast.2, bf16[80,4096]{1,0:T(8,128)(2,1)} %stored.1, f32[64,64]{1,0:T(8,128)} %inv_out.1, ...), custom_call_target="tpu_custom_call" | custom-call | tf_op jit(solution)/shard_map/pallas_call | solution.py:312
  50.1 0.0 copy-done.2
  50.1 0.0 copy-start.1
  50.1 1.2 %copy-done.1 = bf16[4096,128]{1,0:T(8,128)(2,1)S(1)} copy-done((bf16[4096,128]{1,0:T(8,128)(2,1)S(1)}, bf16[4096,128]{1,0:T(8,128)(2,1)}, u32[]{:S(2)}) %copy-start.1) | copy-done | bytes 1048600
  51.3 6.2 %shard_map.83.query = bf16[128,4096]{1,0:T(8,128)(2,1)S(1)} custom-call(bf16[4096,128]{1,0:T(8,128)(2,1)S(1)} %copy-done.1, s32[1,64]{1,0:T(1,128)S(1)} %copy-done.2), custom_call_target="tpu_custom_call" | custom-call | tf_op jit(solution)/shard_map/pallas_call | solution.py:344
  57.5 0.0 copy-start
  57.5 1.3 %copy-done = bf16[160,4096]{1,0:T(8,128)(2,1)S(1)} copy-done((bf16[160,4096]{1,0:T(8,128)(2,1)S(1)}, bf16[160,4096]{1,0:T(8,128)(2,1)}, u32[]{:S(2)}) %copy-start) | copy-done | bytes 1310744
  58.8 3.6 %shard_map.84 = f32[80,128]{1,0:T(8,128)S(1)} custom-call(bf16[160,4096]{1,0:T(8,128)(2,1)S(1)} %copy-done, bf16[128,4096]{1,0:T(8,128)(2,1)S(1)} %shard_map.83.query), custom_call_target="tpu_custom_call" | custom-call | tf_op jit(solution)/shard_map/pallas_call | solution.py:352
  62.5 0.6 copy.10
Async XLA Ops:
  0.0 50.1 %copy-start.2 = (s32[1,64]{1,0:T(1,128)S(1)}, s32[1,64]{1,0:T(1,128)}, u32[]{:S(2)}) copy-start(s32[1,64]{1,0:T(1,128)} %lengths.1) | copy-start | bytes 772
  50.1 1.2 %copy-start.1 = (bf16[4096,128]{1,0:T(8,128)(2,1)S(1)}, bf16[4096,128]{1,0:T(8,128)(2,1)}, u32[]{:S(2)}) copy-start(bf16[4096,128]{1,0:T(8,128)(2,1)} %get-tuple-element.8.tokens) | copy-start | bytes 3145732
  57.5 1.3 %copy-start = (bf16[160,4096]{1,0:T(8,128)(2,1)S(1)}, bf16[160,4096]{1,0:T(8,128)(2,1)}, u32[]{:S(2)}) copy-start(bf16[160,4096]{1,0:T(8,128)(2,1)} %get-tuple-element.7.stored) | copy-start | bytes 3932164
